TPU v7x, 512 devices: a whole 4x8x8 slice. The times are simulated.
512 devices in a mesh: row: 32 (over x, y), col: 16 (over z, core).
Axes of the slice: x: 4, y: 8, z: 8, core: 2. Of those that a mesh axis runs over, the one named last changes fastest.
Arguments:
- grads_out: bfloat16 [1024, 28672], P('row', 'col'), may hold values from -6 to 6
- acts: bfloat16 [1024, 8192], P('col', 'row'), may hold values from -6 to 6
- query_index: int32 [8], replicated, may hold values from 0 to 1023
- train_index: int32 [384], replicated, may hold values from 0 to 1023
- out_basis: bfloat16 [28672, 28672], P('col', 'row'), may hold values from -0.03125 to 0.03125
- in_basis: bfloat16 [8192, 8192], P('row', 'col'), may hold values from -0.0625 to 0.0625
- eig_products: bfloat16 [28672, 8192], P('row', 'col'), may hold values from 0.5 to 200
Outputs:
- scores: float32 [8, 384], replicated
All inputs are finite; a program needn't handle non-finite values.
Results may differ from a plain program's by a relative error of at most 0.0003.
Values may be sent and summed in bfloat16 or wider, within the bound.
A program may use at most 64 MiB of HBM per device.

v0:
```python
import math

import jax
import jax.numpy as jnp
from jax import lax
from jax.sharding import PartitionSpec as P

DOUT = 28672
DIN = 8192


def per_device(grads_out, acts, query_index, train_index, out_basis, in_basis, eig_products):
    wanted = jnp.concatenate([query_index, train_index])
    pool_out = lax.all_gather(grads_out, "row", axis=0, tiled=True)
    pool_in = lax.all_gather(acts, "col", axis=0, tiled=True)
    grad_rows = jnp.take(pool_out, wanted, axis=0)
    act_rows = jnp.take(pool_in, wanted, axis=0)
    out_partial = jnp.dot(grad_rows, out_basis, preferred_element_type=jnp.float32)
    in_partial = jnp.dot(act_rows, in_basis, preferred_element_type=jnp.float32)
    eig_local = jnp.sum(eig_products.astype(jnp.float32))
    out_sums = lax.psum(out_partial, "col")
    in_sums = lax.psum(in_partial, "row")
    eig_total = lax.psum(eig_local, ("row", "col"))
    damping = 0.1 * eig_total / (DOUT * DIN)
    rot_out = out_sums.astype(jnp.bfloat16)
    rot_in = in_sums.astype(jnp.bfloat16)
    inverse = 1.0 / (eig_products.astype(jnp.float32) + damping)
    query_count = query_index.shape[0]
    query_out = rot_out[:query_count].astype(jnp.float32)
    train_out = rot_out[query_count:]
    query_in = rot_in[:query_count].astype(jnp.float32)
    train_in = rot_in[query_count:].astype(jnp.float32)
    normalizer = 1.0 / math.sqrt(DOUT * DIN)
    collected = []
    for query in range(query_count):
        precond = (query_out[query][:, None] * query_in[query][None, :] * inverse).astype(
            jnp.bfloat16
        )
        mixed = jnp.dot(train_out, precond, preferred_element_type=jnp.float32)
        collected.append(lax.psum(jnp.sum(mixed * train_in, axis=1), ("row", "col")))
    totals = jnp.stack(collected)
    return totals * normalizer


def solution(mesh):
    in_specs = (
        P("row", "col"),
        P("col", "row"),
        P(),
        P(),
        P("col", "row"),
        P("row", "col"),
        P("row", "col"),
    )
    out_specs = P()
    return jax.shard_map(
        per_device, mesh=mesh, in_specs=in_specs, out_specs=out_specs, check_vma=False
    )
```

profile of v0, /device:TPU:1, one launch (start us, length us, event | category | flops | bytes accessed | tf_op | source)
XLA Modules:
  0.0 470.5 jit_solution(4086505755431920079)
XLA Ops:
  6.5 0.7 all-gather.2.cloned.1.call-update
  7.3 2.4 convert_reduce_fusion
  9.6 107.5 %psum.79 = f32[]{:T(128)} all-reduce(f32[]{:T(128)} %convert_reduce_fusion), channel_id=1, replica_groups=mesh['row'=32,'col'=16] {'row','col'}, use_global_device_ids=true, to_apply=%region_3.4 | all-reduce | flops 1 | bytes 8 | tf_op jit(solution)/shard_map/psum | solution.py:23
  117.1 0.7 concatenate.32
  117.8 0.7 compare_select_fusion
  118.5 19.1 %all_gather.7 = bf16[1024,256]{1,0:T(8,128)(2,1)} all-gather(bf16[64,256]{1,0:T(8,128)(2,1)} %param.8), channel_id=1, replica_groups=mesh['row'=32,'col'=16] {'col'}, dimensions={0}, use_global_device_ids=true | all-gather | bytes 557056 | tf_op jit(solution)/shard_map/all_gather | solution.py:15
  137.6 2.8 gather_fusion.1
  140.5 2.2 fusion.29
  143.3 121.1 %all-reduce.4 = bf16[392,512]{1,0:T(8,128)(2,1)} all-reduce(f32[392,512]{1,0:T(8,128)} %fusion.29), channel_id=1, replica_groups=mesh['row'=32,'col'=16] {'row'}, use_global_device_ids=true, to_apply=%region_1.2 | all-reduce | flops 200704 | bytes 1204224 | tf_op jit(solution)/shard_map/psum | solution.py:22
  264.4 0.7 slice_convert_fusion.1
  265.2 7.1 %gather_fusion = bf16[392,1792]{1,0:T(8,128)(2,1)} fusion(bf16[1024,1792]{1,0:T(8,128)(2,1)} %all-gather.2.cloned.1.call-done, s32[1024]{0:T(1024)S(1)} %pad_clamp_fusion), kind=kCustom, calls=%fused_computation | custom fusion | bytes 2811424 | tf_op jit(solution)/shard_map/jit(_take)/gather | solution.py:16
  272.3 4.2 fusion.1
  276.5 82.5 %all-reduce.3 = bf16[392,896]{1,0:T(8,128)(2,1)} all-reduce(f32[392,896]{1,0:T(8,128)} %fusion.1), channel_id=1, replica_groups=mesh['row'=32,'col'=16] {'col'}, use_global_device_ids=true, to_apply=%region_0.1 | all-reduce | flops 351232 | bytes 2107392 | tf_op jit(solution)/shard_map/psum | solution.py:21
  359.0 0.7 slice_convert_fusion
  359.8 2.4 fusion.11
  362.2 0.7 fusion.10
  363.0 0.8 fusion.9
  363.8 0.7 fusion.8
  364.5 0.8 fusion.7
  365.3 0.8 fusion.6
  366.0 0.8 fusion.5
  366.8 0.7 fusion.4
  367.5 95.5 %all-reduce = (f32[1,384]{1,0:T(1,128)S(1)}, f32[1,384]{1,0:T(1,128)S(1)}, f32[1,384]{1,0:T(1,128)S(1)}, f32[1,384]{1,0:T(1,128)S(1)}, f32[1,384]{1,0:T(1,128)S(...) all-reduce(f32[1,384]{1,0:T(1,128)S(1)} %stack.27, ...), channel_id=1, replica_groups=mesh['row'=32,'col'=16] {'row','col'}, use_global_device_ids=true, to_apply=%region_5.6 | all-reduce | flops 3072 | bytes 24576 | tf_op jit(solution)/shard_map/psum | solution.py:40
  463.1 0.6 broadcast_multiply_fusion
  (27 shorter events, 0.3 us)
Async XLA Ops:
  6.5 265.8 %copy-start = (bf16[1792,896]{1,0:T(8,128)(2,1)S(1)}, bf16[1792,896]{1,0:T(8,128)(2,1)}, u32[]{:S(2)}) copy-start(bf16[1792,896]{1,0:T(8,128)(2,1)} %param.11) | copy-start | bytes 9633796
  6.5 133.9 %copy-start.4 = (s32[384]{0:T(512)S(1)}, s32[384]{0:T(512)}, u32[]{:S(2)}) copy-start(s32[384]{0:T(512)} %param.10) | copy-start | bytes 4612
  6.5 133.9 %copy-start.5 = (s32[8]{0:T(128)S(1)}, s32[8]{0:T(128)}, u32[]{:S(2)}) copy-start(s32[8]{0:T(128)} %param.9) | copy-start | bytes 100
  6.5 258.6 %all-gather.2.cloned.1.call-start = ((), (), s32[]{:S(2)}) async-start(), calls=%async_computation | async-start | bytes 3784704 | tf_op jit(solution)/shard_map/all_gather | solution.py:14
  359.8 2.4 copy-start.1
  359.8 2.4 copy-start.2
  359.8 2.4 copy-start.3
Sparse Core Ops, SparseCore 0:
  10.5 88.3 all-gather.1
where the time goes:
time: 471 us
  blocking collectives  426 us (90%)
  between operations  14.2 us (3%)
  matrix products  14 us (3%)
  local copies, waits for them, and re-layouts  10.8 us (2%)
  other arithmetic  5.21 us (1%)
    psum x1, blocking collectives, per_device(): in_sums = lax.psum(in_partial, 'row')  121 us
    psum x1, blocking collectives, per_device(): eig_total = lax.psum(eig_local, ('row', 'col'))  107 us
    psum x1, blocking collectives, per_device(): lax.psum(jnp.sum(mixed * train_in, axis=1), ('row', 'col'))  95.5 us
    psum x1, blocking collectives, per_device(): out_sums = lax.psum(out_partial, 'col')  82.5 us
    all_gather x1, blocking collectives, per_device(): pool_in = lax.all_gather(acts, 'col', axis=0, tiled=True)  19.1 us
  transfers between devices with their start and end apart: 1, of which 0 were waited for; matrix products, arithmetic and copies ran while one was open for 2% of the time, Pallas kernels for 0%

commit v1 on v0

v1 whole, which is shorter than its diff:
```python
import math

import jax
import jax.numpy as jnp
from jax import lax
from jax.experimental import pallas as pl
from jax.experimental.pallas import tpu as pltpu
from jax.sharding import PartitionSpec as P

DOUT = 28672
DIN = 8192
QUERIES = 8
TRAIN = 384
POOL = 1024
X, Y, Z = 4, 8, 8
PICKS = 400
CA = 768
CB = 1024
IB = 896
JB = 512
TCH = 48
CH = 56
MESH = pl.DeviceIdType.MESH
F32 = jnp.float32
BF16 = jnp.bfloat16
PARTS = ((0, 24), (24, 32))
N_SEM = 144


def kernel(
    wanted, grads, acts, out_basis, in_basis, eig, out,
    pool_a, pool_b, pool_c, hot_a, hot_b, hot_c, obv, ibv, eigv, inverse, picked,
    part, swap, ringbuf, sendbuf, own, own_other, rout, rquery,
    in_part, in_x, in_sum, in_y, rin, damp_s, damp_z, damp_y, damp_x,
    fin_s, fin_z, fin_y, fin_x, send_sems, recv_sems, load_sems,
):
    row = lax.axis_index("row")
    col = lax.axis_index("col")
    x, y = row // Y, row % Y
    z, k = col // 2, col % 2
    other = 1 - k
    turn = 1 - 2 * k

    def dev(ox=0, oy=0, oz=0):
        return (((x + ox + X) % X) * Y + (y + oy + Y) % Y, ((z + oz + Z) % Z) * 2 + k)

    sibling = (row, z * 2 + other)
    used = [0]
    pending = []

    def remote(src, dst, target, start=True):
        at = used[0]
        used[0] += 1
        copy = pltpu.make_async_remote_copy(
            src_ref=src, dst_ref=dst, send_sem=send_sems.at[at], recv_sem=recv_sems.at[at],
            device_id=target, device_id_type=MESH,
        )
        if start:
            copy.start()
            pending.append(copy)
        return copy

    def rows(start, size):
        return pl.ds(pl.multiple_of(start, 8), size)

    def at_a(px, py):
        return pl.ds(pl.multiple_of(((py + Y) % Y) * 128 + ((px + X) % X) * 32, 32), 32)

    def at_b(px, py, size=32, skip=0):
        return pl.ds(pl.multiple_of(((px + X) % X) * 256 + ((py + Y) % Y) * 32 + skip, 16), size)

    def at_a_group(py, size=128, skip=0):
        return pl.ds(pl.multiple_of(((py + Y) % Y) * 128 + skip, 32), size)

    own_c = pl.ds(pl.multiple_of(k * 512 + z * 64, 64), 64)
    loads = [
        pltpu.make_async_copy(grads.at[:, pl.ds(CA, CB)], pool_b.at[at_b(x, y)], load_sems.at[0]),
        pltpu.make_async_copy(grads.at[:, pl.ds(0, CA)], pool_a.at[at_a(x, y)], load_sems.at[1]),
        pltpu.make_async_copy(acts, pool_c.at[own_c], load_sems.at[2]),
        pltpu.make_async_copy(eig, eigv, load_sems.at[3]),
        pltpu.make_async_copy(in_basis, ibv, load_sems.at[4]),
        pltpu.make_async_copy(out_basis, obv, load_sems.at[5]),
    ]
    for load in loads:
        load.start()

    @pl.when(k == 1)
    def _():
        ringbuf[0] = jnp.zeros((CH, IB), F32)

    barrier = pltpu.get_barrier_semaphore()
    partners = [sibling]
    partners += [dev(oz=o) for o in range(1, Z)]
    partners += [dev(oy=o) for o in range(1, Y)]
    partners += [dev(ox=o) for o in range(1, X)]
    for partner in partners:
        pl.semaphore_signal(barrier, inc=1, device_id=partner, device_id_type=MESH)
    for load in loads[:3]:
        load.wait()
    pl.semaphore_wait(barrier, len(partners))

    def go(buf, where, **to):
        return remote(buf.at[where], buf.at[where], dev(**to))

    b_y = {}
    b_x = {}
    b_x2 = {}
    a_y = {}
    b_y[1] = [go(pool_b, at_b(x, y), oy=1), go(pool_b, at_b(x, y), oy=-1)]
    a_x = [go(pool_a, at_a(x, y), ox=o) for o in (1, 3, 2)]
    b_x[0] = [go(pool_b, at_b(x, y), ox=1), go(pool_b, at_b(x, y), ox=-1)]
    a_y[1] = [go(pool_a, at_a(x, y), oy=1), go(pool_a, at_a(x, y), oy=-1)]
    c_z = [go(pool_c, own_c, oz=o) for o in (1, 7, 2, 6, 3, 5, 4)]

    loads[3].wait()
    total = jnp.zeros((8, 128), F32)
    for at in range(0, IB, 128):
        block = eigv[at:at + 128, :].astype(F32)
        for at_lane in range(0, JB, 128):
            total = total + jnp.sum(block[:, at_lane:at_lane + 128].reshape(16, 8, 128), axis=0)

    def sum_start(buf, me, value, targets):
        buf[me] = value
        return [remote(buf.at[me], buf.at[me], target) for target in targets]

    def sum_end(buf, copies):
        for copy in copies:
            copy.wait_recv()
        result = buf[0]
        for at in range(1, buf.shape[0]):
            result = result + buf[at]
        return result

    to_z = [dev(oz=o) for o in range(1, Z)]
    to_y = [dev(oy=o) for o in range(1, Y)]
    to_x = [dev(ox=o) for o in range(1, X)]
    damp = sum_start(damp_s, k, total, [sibling])

    want = wanted[...]
    place = lax.broadcasted_iota(jnp.int32, (PICKS, POOL), 1)
    hot_b[...] = (place == want).astype(F32).astype(BF16)
    hot_a[...] = (((place // 32) % 4) * 256 + (place // 128) * 32 + place % 32 == want).astype(F32).astype(BF16)
    hot_c[...] = (((place // 64) % 8) * 128 + (place // 512) * 64 + place % 64 == want).astype(F32).astype(BF16)

    for copy in b_y[1]:
        copy.wait_recv()
    b_y[2] = [go(pool_b, at_b(x, y - 1), oy=1), go(pool_b, at_b(x, y + 1), oy=-1)]
    for j in (-1, 1):
        b_x[j] = [go(pool_b, at_b(x, y + j), ox=1), go(pool_b, at_b(x, y + j), ox=-1)]
    for o, copy in zip((1, 3, 2), a_x):
        copy.wait_recv()
        a_y[1] += [go(pool_a, at_a(x - o, y), oy=1), go(pool_a, at_a(x - o, y), oy=-1)]
    damp = sum_start(damp_z, z, sum_end(damp_s, damp), to_z)

    for copy in b_y[2]:
        copy.wait_recv()
    b_y[3] = [go(pool_b, at_b(x, y - 2), oy=1), go(pool_b, at_b(x, y + 2), oy=-1)]
    for j in (-2, 2):
        b_x[j] = [go(pool_b, at_b(x, y + j), ox=1), go(pool_b, at_b(x, y + j), ox=-1)]
    for copy in a_y[1]:
        copy.wait_recv()
    a_y[2] = [go(pool_a, at_a_group(y - 1), oy=1), go(pool_a, at_a_group(y + 1), oy=-1)]

    def b_cross(j):
        for copy in b_x[j]:
            copy.wait_recv()
        if j in (0, 1, 2, 3):
            b_x2[j] = go(pool_b, at_b(x - 1, y + j), ox=1)
        else:
            b_x2[j] = go(pool_b, at_b(x + 1, y + j), ox=-1)

    b_cross(0)
    for copy in c_z:
        copy.wait_recv()
    half_c = pl.ds(pl.multiple_of(k * 512, 512), 512)
    c_s = remote(pool_c.at[half_c], pool_c.at[half_c], sibling)
    damp = sum_start(damp_y, y, sum_end(damp_z, damp), to_y)

    for copy in b_y[3]:
        copy.wait_recv()
    b_y[4] = [
        remote(pool_b.at[at_b(x, y - 3, 16)], pool_b.at[at_b(x, y - 3, 16)], dev(oy=1)),
        remote(pool_b.at[at_b(x, y + 3, 16, 16)], pool_b.at[at_b(x, y + 3, 16, 16)], dev(oy=-1)),
    ]
    for j in (-3, 3):
        b_x[j] = [go(pool_b, at_b(x, y + j), ox=1), go(pool_b, at_b(x, y + j), ox=-1)]
    for copy in a_y[2]:
        copy.wait_recv()
    a_y[3] = [go(pool_a, at_a_group(y - 2), oy=1), go(pool_a, at_a_group(y + 2), oy=-1)]
    b_cross(1)
    b_cross(-1)

    c_s.wait_recv()
    loads[4].wait()
    act_rows = jnp.dot(hot_c[...], pool_c[...], preferred_element_type=F32).astype(BF16)
    for at in range(X):
        in_part[at] = jnp.dot(act_rows, ibv[:, at * 128:at * 128 + 128], preferred_element_type=F32)

    for copy in b_y[4]:
        copy.wait_recv()
    b_x[4] = [go(pool_b, at_b(x, y + 4), ox=1), go(pool_b, at_b(x, y + 4), ox=-1)]
    for copy in a_y[3]:
        copy.wait_recv()
    a_y[4] = [
        go(pool_a, at_a_group(y - 3, 64), oy=1),
        go(pool_a, at_a_group(y + 3, 64, 64), oy=-1),
    ]
    for j in (2, -2, 3, -3, 4):
        b_cross(j)
    damp = sum_start(damp_x, x, sum_end(damp_y, damp), to_x)

    in_copies = [
        remote(in_part.at[(x + o) % X], in_x.at[o - 1], dev(ox=o)) for o in range(1, X)
    ]

    for copy in a_y[4]:
        copy.wait_recv()
    for at in range(0, CA, 256):
        picked[:, at:at + 256] = jnp.dot(
            hot_a[...], pool_a[:, at:at + 256], preferred_element_type=F32
        ).astype(BF16)
    for j in b_x2:
        b_x2[j].wait_recv()
    for at in range(0, CB, 256):
        picked[:, CA + at:CA + at + 256] = jnp.dot(
            hot_b[...], pool_b[:, at:at + 256], preferred_element_type=F32
        ).astype(BF16)
    loads[5].wait()
    for at in range(0, IB, 256):
        width = min(256, IB - at)
        rotated = jnp.dot(picked[...], obv[:, at:at + width], preferred_element_type=F32)
        for d in range(Z):
            part[d * CH:d * CH + TCH, at:at + width] = rotated[d * TCH:d * TCH + TCH]
            part[d * CH + TCH:d * CH + CH, at:at + width] = rotated[TRAIN:TRAIN + QUERIES]

    def chunk(d):
        return rows(((d + 2 * Z) % Z) * CH, CH)

    swaps = []
    for j in range(4):
        need = jnp.where(k == 1, z + 4 - j, z if j == 0 else z - 4 + j)
        swaps.append(remote(part.at[chunk(need)], swap.at[j], sibling))

    hops = []
    for s in range(4):
        swaps[s].wait_recv()
        mine = part.at[chunk(z + turn * (4 - s))]
        hop = []
        for p, (first, size) in enumerate(PARTS):
            span = pl.ds(first, size)
            if s > 0:
                if s == 1:
                    @pl.when(k == 0)
                    def _():
                        hops[0][p].wait_recv()
                else:
                    hops[s - 1][p].wait_recv()
                sendbuf[s, span] = mine[span] + swap[s, span] + ringbuf[s - 1, span]
            else:
                sendbuf[s, span] = mine[span] + swap[s, span]
            copy = remote(
                sendbuf.at[s, span], ringbuf.at[s, span], dev(oz=turn), start=s > 0
            )
            if s == 0:
                @pl.when(k == 0)
                def _():
                    copy.start()
            hop.append(copy)
        hops.append(hop)
        if s == 1:
            for copy in in_copies:
                copy.wait_recv()
            sums = in_part[x]
            for o in range(1, X):
                sums = sums + in_x[o - 1]
            for d in range(Y):
                in_sum[d, 0:TCH] = sums[d * TCH:d * TCH + TCH]
                in_sum[d, TCH:CH] = sums[TRAIN:TRAIN + QUERIES]
            in_copies = [
                remote(in_sum.at[(y + o) % Y], in_y.at[o - 1], dev(oy=o)) for o in range(1, Y)
            ]
        if s == 2:
            damping = 0.1 * jnp.sum(sum_end(damp_x, damp)) / (DOUT * DIN)
            inverse[...] = 1.0 / (eigv[...].astype(F32) + damping)

    def in_middle():
        for copy in in_copies:
            copy.wait_recv()
        sums = in_sum[y]
        for o in range(1, Y):
            sums = sums + in_y[o - 1]
        rin[x, pl.ds(pl.multiple_of(y * TCH, 16), TCH)] = sums[0:TCH].astype(BF16)
        rin[x, TRAIN:PICKS] = jnp.concatenate([sums[TCH:CH], sums[TCH:CH]], axis=0).astype(BF16)
        span = pl.ds(pl.multiple_of(y * TCH, 16), TCH)
        return [remote(rin.at[x, span], rin.at[x, span], dev(oy=o)) for o in range(1, Y)]

    for p, (first, size) in enumerate(PARTS):
        span = pl.ds(first, size)
        hops[3][p].wait_recv()
        rest = part[rows(z * CH + first, size)] + swap[0, span]
        own[span] = ringbuf[3, span] + jnp.where(k == 1, rest, 0.0)
    meet = remote(own, own_other, sibling)
    in_copies = in_middle()
    meet.wait_recv()
    full = own[...] + own_other[...]
    rquery[...] = full[TCH:CH].astype(BF16).astype(F32)
    mine = pl.ds(pl.multiple_of(z * TCH, 16), TCH)
    rout[mine] = full[0:TCH].astype(BF16)

    spread = []
    for o in (4, 1, 2, 3):
        copy = remote(rout.at[mine], rout.at[mine], dev(oz=turn * o), start=o < 4)
        if o == 4:
            @pl.when(k == 0)
            def _():
                copy.start()
        spread.append((o, copy))

    for copy in in_copies:
        copy.wait_recv()
    in_copies = [remote(rin.at[x], rin.at[x], dev(ox=o)) for o in range(1, X)]

    across = []
    for o, copy in spread[1:] + spread[:1]:
        span = pl.ds(pl.multiple_of(((z - turn * o + Z) % Z) * TCH, 16), TCH)
        relay = remote(rout.at[span], rout.at[span], sibling, start=False)
        if o < 4:
            copy.wait_recv()
            relay.start()
            pending.append(relay)
        else:
            @pl.when(k == 0)
            def _():
                copy.wait_recv()
                relay.start()
        across.append((o, copy, relay))
    for copy in in_copies:
        copy.wait_recv()
    for o, copy, relay in across:
        if o < 4:
            relay.wait_recv()
        else:
            @pl.when(k == 1)
            def _():
                relay.wait_recv()

    query_columns = jnp.transpose(rquery[...])
    lanes = lax.broadcasted_iota(jnp.int32, (TRAIN, 128), 1)
    collected = jnp.zeros((TRAIN, 128), F32)
    for q in range(QUERIES):
        column = query_columns[:, q:q + 1]
        total = jnp.zeros((TRAIN, 128), F32)
        for at in range(0, X, 2):
            halves = []
            for t in (at, at + 1):
                line = rin[t, TRAIN:PICKS].astype(F32)[q:q + 1]
                halves.append((column * line * inverse[:, t * 128:t * 128 + 128]).astype(BF16))
            mixed = jnp.dot(rout[...], jnp.concatenate(halves, axis=1), preferred_element_type=F32)
            for n, t in enumerate((at, at + 1)):
                total = total + mixed[:, n * 128:n * 128 + 128] * rin[t, 0:TRAIN].astype(F32)
        collected = jnp.where(lanes == q, jnp.sum(total, axis=1, keepdims=True), collected)
    scores = jnp.transpose(collected)[0:QUERIES]

    fin = sum_start(fin_s, k, scores, [sibling])
    fin = sum_start(fin_z, z, sum_end(fin_s, fin), to_z)
    fin = sum_start(fin_y, y, sum_end(fin_z, fin), to_y)
    fin = sum_start(fin_x, x, sum_end(fin_y, fin), to_x)
    out[...] = sum_end(fin_x, fin) * (1.0 / math.sqrt(DOUT * DIN))

    for copy in pending:
        copy.wait_send()

    @pl.when(k == 0)
    def _():
        for copy in hops[0] + [spread[0][1], across[-1][2]]:
            copy.wait_send()


def per_device(grads_out, acts, query_index, train_index, out_basis, in_basis, eig_products):
    padding = jnp.full((PICKS - TRAIN - QUERIES,), -1, jnp.int32)
    wanted = jnp.concatenate([train_index, query_index, padding])[:, None]
    vmem = pl.BlockSpec(memory_space=pltpu.VMEM)
    hbm = pl.BlockSpec(memory_space=pl.ANY)
    return pl.pallas_call(
        kernel,
        out_shape=jax.ShapeDtypeStruct((QUERIES, TRAIN), F32),
        in_specs=[vmem] + [hbm] * 5,
        out_specs=vmem,
        scratch_shapes=[
            pltpu.VMEM((POOL, CA), BF16),
            pltpu.VMEM((POOL, CB), BF16),
            pltpu.VMEM((POOL, 256), BF16),
            pltpu.VMEM((PICKS, POOL), BF16),
            pltpu.VMEM((PICKS, POOL), BF16),
            pltpu.VMEM((PICKS, POOL), BF16),
            pltpu.VMEM((CA + CB, IB), BF16),
            pltpu.VMEM((256, JB), BF16),
            pltpu.VMEM((IB, JB), BF16),
            pltpu.VMEM((IB, JB), F32),
            pltpu.VMEM((PICKS, CA + CB), BF16),
            pltpu.VMEM((Z * CH, IB), F32),
            pltpu.VMEM((4, CH, IB), F32),
            pltpu.VMEM((4, CH, IB), F32),
            pltpu.VMEM((4, CH, IB), F32),
            pltpu.VMEM((CH, IB), F32),
            pltpu.VMEM((CH, IB), F32),
            pltpu.VMEM((TRAIN, IB), BF16),
            pltpu.VMEM((QUERIES, IB), F32),
            pltpu.VMEM((X, PICKS, 128), F32),
            pltpu.VMEM((X - 1, PICKS, 128), F32),
            pltpu.VMEM((Y, CH, 128), F32),
            pltpu.VMEM((Y - 1, CH, 128), F32),
            pltpu.VMEM((X, PICKS, 128), BF16),
            pltpu.VMEM((2, 8, 128), F32),
            pltpu.VMEM((Z, 8, 128), F32),
            pltpu.VMEM((Y, 8, 128), F32),
            pltpu.VMEM((X, 8, 128), F32),
            pltpu.VMEM((2, QUERIES, TRAIN), F32),
            pltpu.VMEM((Z, QUERIES, TRAIN), F32),
            pltpu.VMEM((Y, QUERIES, TRAIN), F32),
            pltpu.VMEM((X, QUERIES, TRAIN), F32),
            pltpu.SemaphoreType.DMA((N_SEM,)),
            pltpu.SemaphoreType.DMA((N_SEM,)),
            pltpu.SemaphoreType.DMA((6,)),
        ],
        compiler_params=pltpu.CompilerParams(
            collective_id=0, has_side_effects=True, vmem_limit_bytes=56 * 2**20
        ),
    )(wanted, grads_out, acts, out_basis, in_basis, eig_products)


def solution(mesh):
    in_specs = (
        P("row", "col"),
        P("col", "row"),
        P(),
        P(),
        P("col", "row"),
        P("row", "col"),
        P("row", "col"),
    )
    return jax.shard_map(
        per_device, mesh=mesh, in_specs=in_specs, out_specs=P(), check_vma=False
    )
```

time: 471 us -> 102 us (0.22)
  blocking collectives: 426 us -> 0 us
  Pallas kernels: 0 us -> 98.4 us
  between operations: 14.2 us -> 0.01 us
  matrix products: 14 us -> 0 us
  local copies, waits for them, and re-layouts: 10.8 us -> 2.13 us
    psum x4 -> x0, blocking collectives: 407 us -> none  [the longest x1 121 us: per_device(): in_sums = lax.psum(in_partial, 'row')]
    pallas_call x0 -> x1, Pallas kernels: none -> 98.4 us  [per_device(): pl.pallas_call(kernel, out_shape=jax.ShapeDtypeStruct((QUERIES, TRAIN), F...]
    all_gather x1 -> x0, blocking collectives: 19.1 us -> none  [per_device(): pool_in = lax.all_gather(acts, 'col', axis=0, tiled=True)]
    dot_general x10 -> x0, matrix products: 14 us -> none  [the longest x8 7.63 us: per_device(): mixed = jnp.dot(train_out, precond, preferred_element_type=jnp.float32)]
    gather x2 -> x0, local copies, waits for them, and re-layouts: 9.91 us -> none  [the longest x1 7.12 us: per_device(): grad_rows = jnp.take(pool_out, wanted, axis=0)]
  transfers between devices with their start and end apart: 1 -> 0, of which waited for: 0 -> 0; matrix products, arithmetic and copies ran while one was open for 2% -> 0% of each run, Pallas kernels for 0% -> 0%
where the time goes in v1:
time: 102 us; the launch traced here: 101 us
  Pallas kernels  98.4 us (96%)
  local copies, waits for them, and re-layouts  2.13 us (2%)
    pallas_call x1, Pallas kernels, per_device(): pl.pallas_call(kernel, out_shape=jax.ShapeDtypeStruct((QUERIES, TRAIN), F...  98.4 us

profile of v1, /device:TPU:1, one launch (start us, length us, event | category | flops | bytes accessed | tf_op | source)
XLA Modules:
  0.0 101.3 jit_solution(18222322075289326775)
XLA Ops:
  0.0 0.8 pad_add_fusion
  0.8 0.8 copy.8.wanted
  1.6 98.4 %shard_map.73 = f32[8,384]{1,0:T(8,128)} custom-call(s32[400,1]{1,0:T(8,128)} %copy.8.wanted, bf16[32,1792]{1,0:T(8,128)(2,1)} %grads.1, bf16[64,256]{1,0:T(8,128)(2,1)} %acts.1, bf16[1792,896]{1,0:T(8,128)(2,1)} %out_basis.1, bf16[256,512]{1,0:T(8,128)(2,1)} %in_basis.1, bf16[896,512]{1,0:T(8,128)(2,1)} %eig.1), custom_call_target="tpu_custom_call" | custom-call | tf_op jit(solution)/shard_map/pallas_call | solution.py:384
  100.0 1.3 %copy.10 = f32[8,384]{1,0:T(8,128)} copy(f32[8,384]{1,0:T(8,128)} %shard_map.73) | data formatting | bytes 24576
  (1 shorter events, 0.0 us)

commit v2 on v1

v2 whole, which is shorter than its diff:
```python
import math

import jax
import jax.numpy as jnp
from jax import lax
from jax.experimental import pallas as pl
from jax.experimental.pallas import tpu as pltpu
from jax.sharding import PartitionSpec as P

DOUT = 28672
DIN = 8192
QUERIES = 8
TRAIN = 384
POOL = 1024
X, Y, Z = 4, 8, 8
PICKS = 400
CA = 768
CB = 1024
IB = 896
JB = 512
TCH = 48
CH = 56
MESH = pl.DeviceIdType.MESH
F32 = jnp.float32
BF16 = jnp.bfloat16
PARTS = ((0, 16), (16, 16), (32, 24))
N_SEM = 208
ORDER = (
    ('A', 0, 1), ('A', 0, 3), ('B', 1), ('B', -1), ('Bx', 0, -1), ('eig',), ('A', 0, 2), ('Bx', 0, 1),
    ('B', 2), ('B', -2), ('A', 1, 0), ('A', -1, 0), ('damp_z',), ('A', 1, 1), ('A', -1, 1), ('Bx', 1, 1),
    ('Bx', 1, -1), ('A', 1, 3), ('A', -1, 3), ('hot_c',), ('Bx', -1, 1), ('Bx', -1, -1), ('hot_b',),
    ('A', 1, 2), ('A', -1, 2), ('Bxx', 0), ('acts',), ('Bx', 2, -1), ('B', 3), ('B', -3), ('Bx', 2, 1),
    ('Bx', -2, -1), ('damp_y',), ('B', 4), ('B', -4), ('Bx', -2, 1), ('A', 2, 0), ('A', -2, 0), ('A', 2, 1),
    ('A', -2, 1), ('Bxx', 1), ('in_rot',), ('Bxx', -1), ('A', 2, 3), ('A', -2, 3), ('A', 2, 2), ('A', -2, 2),
    ('hot_a',), ('Bx', 3, 1), ('pick_b', 0), ('Bx', 3, -1), ('Bx', -3, 1), ('Bx', -3, -1), ('A', 3, 0),
    ('A', -3, 0), ('Bxx', 2), ('Bxx', -2), ('A', 3, 1), ('A', -3, 1), ('Bx', 4, 1), ('Bx', 4, -1),
    ('damp_x',), ('A', 3, 3), ('Bx', -4, 1), ('Bx', -4, -1), ('pick_b', 1), ('pick_b', 3), ('A', -3, 3),
    ('A', 3, 2), ('A', -3, 2), ('Bxx', 3), ('in_x',), ('A', 4, 0), ('A', -4, 0), ('Bxx', -3), ('A', 4, 1),
    ('A', -4, 1), ('Bxx', 4), ('A', 4, 3), ('A', -4, 3), ('Bxx', -4), ('A', 4, 2), ('A', -4, 2),
)


def kernel(
    train_index, query_index, grads, acts, out_basis, in_basis, eig, out,
    want_rows, pool_a, pool_b, pool_c, sum_b, hot_a, hot_b, hot_c, obv, ibv, eigv, inverse, picked,
    part, swap, ringbuf, sendbuf, own, own_other, rout, rquery,
    in_part, in_relay, in_send, in_x, in_sum, in_y, rin, rin_query, precond, damp_s, damp_z, damp_y, damp_x,
    fin_s, fin_z, fin_y, fin_x, send_sems, recv_sems, load_sems,
):
    row = lax.axis_index("row")
    col = lax.axis_index("col")
    x, y = row // Y, row % Y
    z, k = col // 2, col % 2
    other = 1 - k
    turn = 1 - 2 * k

    def dev(ox=0, oy=0, oz=0):
        return (((x + ox + X) % X) * Y + (y + oy + Y) % Y, ((z + oz + Z) % Z) * 2 + k)

    sibling = (row, z * 2 + other)
    used = [0]
    pending = []

    def remote(src, dst, target, start=True):
        at = used[0]
        used[0] += 1
        copy = pltpu.make_async_remote_copy(
            src_ref=src, dst_ref=dst, send_sem=send_sems.at[at], recv_sem=recv_sems.at[at],
            device_id=target, device_id_type=MESH,
        )
        if start:
            copy.start()
            pending.append(copy)
        return copy

    def rows(start, size):
        return pl.ds(pl.multiple_of(start, 8), size)

    barrier = pltpu.get_barrier_semaphore()
    partners = [sibling]
    partners += [dev(oz=o) for o in range(1, Z)]
    partners += [dev(oy=o) for o in range(1, Y)]
    partners += [dev(ox=o) for o in range(1, X)]
    for partner in partners:
        pl.semaphore_signal(barrier, inc=1, device_id=partner, device_id_type=MESH)

    def at_a(px, py):
        return pl.ds(pl.multiple_of(((py + Y) % Y) * 128 + ((px + X) % X) * 32, 32), 32)

    def at_b(px, py, size=32, skip=0):
        return pl.ds(pl.multiple_of(((px + X) % X) * 256 + ((py + Y) % Y) * 32 + skip, 16), size)

    own_c = pl.ds(pl.multiple_of(k * 512 + z * 64, 64), 64)
    loads = [
        pltpu.make_async_copy(grads.at[:, pl.ds(CA, CB)], pool_b.at[at_b(x, y)], load_sems.at[0]),
        pltpu.make_async_copy(grads.at[:, pl.ds(0, CA)], pool_a.at[at_a(x, y)], load_sems.at[1]),
        pltpu.make_async_copy(acts, pool_c.at[own_c], load_sems.at[2]),
        pltpu.make_async_copy(eig, eigv, load_sems.at[3]),
        pltpu.make_async_copy(in_basis, ibv, load_sems.at[4]),
        pltpu.make_async_copy(out_basis, obv, load_sems.at[5]),
    ]
    for load in loads[:4]:
        load.start()

    @pl.when(k == 1)
    def _():
        ringbuf[0] = jnp.zeros((CH, IB), F32)

    for load in loads[:3]:
        load.wait()
    pl.semaphore_wait(barrier, len(partners))

    coming = {}

    def go(event, buf, where, **to):
        coming[event] = remote(buf.at[where], buf.at[where], dev(**to))

    def block_b(px, d):
        if abs(d) == 4:
            return at_b(px, y - 4, 16, 0 if d > 0 else 16)
        return at_b(px, y - d)

    def on_b(d):
        if abs(d) == 2:
            s = d // 2
            go(("B", 3 * s), pool_b, at_b(x, y - d), oy=s)
            go(("B", 4 * s), pool_b, at_b(x, y - d, 16, 0 if s > 0 else 16), oy=2 * s)
        go(("Bx", d, 1), pool_b, block_b(x, d), ox=1)
        go(("Bx", d, -1), pool_b, block_b(x, d), ox=-1)

    def on_bx(d, s):
        if (s > 0) == (d in (0, 1, 2, 3)):
            go(("Bxx", d), pool_b, block_b(x - s, d), ox=s)

    def on_a(d, o):
        where = at_a(x - o, y - d)
        if d == 0:
            go(("A", 1, o), pool_a, where, oy=1)
            go(("A", -1, o), pool_a, where, oy=-1)
        elif abs(d) < 3:
            s = 1 if d > 0 else -1
            go(("A", d + s, o), pool_a, where, oy=s)
        elif abs(d) == 3 and (d > 0) == (o < 2):
            s = d // 3
            go(("A", 4 * s, o), pool_a, where, oy=s)

    go(("B", 1), pool_b, at_b(x, y), oy=1)
    go(("B", -1), pool_b, at_b(x, y), oy=-1)
    for o in (1, 3, 2):
        go(("A", 0, o), pool_a, at_a(x, y), ox=o)
    go(("B", 2), pool_b, at_b(x, y), oy=2)
    go(("B", -2), pool_b, at_b(x, y), oy=-2)
    on_a(0, 0)
    go(("Bx", 0, 1), pool_b, at_b(x, y), ox=1)
    go(("Bx", 0, -1), pool_b, at_b(x, y), ox=-1)
    c_z = [remote(pool_c.at[own_c], pool_c.at[own_c], dev(oz=o)) for o in (1, 7, 2, 6, 3, 5, 4)]
    for load in loads[4:]:
        load.start()

    def sum_start(buf, me, value, targets):
        buf[me] = value
        return [remote(buf.at[me], buf.at[me], target) for target in targets]

    def sum_end(buf, copies):
        for copy in copies:
            copy.wait_recv()
        result = buf[0]
        for at in range(1, buf.shape[0]):
            result = result + buf[at]
        return result

    to_z = [dev(oz=o) for o in range(1, Z)]
    to_y = [dev(oy=o) for o in range(1, Y)]
    to_x = [dev(ox=o) for o in range(1, X)]

    train_line = jnp.broadcast_to(train_index[...].reshape(1, TRAIN).astype(F32), (8, TRAIN))
    want_rows[0:TRAIN] = jnp.transpose(train_line)[:, 0:1].astype(jnp.int32)
    lines = lax.broadcasted_iota(jnp.int32, (PICKS - TRAIN, 1), 0)
    query_rows = jnp.full((PICKS - TRAIN, 1), -1, jnp.int32)
    for q in range(QUERIES):
        query_rows = jnp.where(lines == q, query_index[q], query_rows)
    want_rows[TRAIN:PICKS] = query_rows

    def mark(hot, order):
        place = lax.broadcasted_iota(jnp.int32, (PICKS, POOL), 1)
        hot[...] = (order(place) == want_rows[...]).astype(F32).astype(BF16)

    def pick_b(o, last=False):
        group = pl.ds(pl.multiple_of(((x + X - o) % X) * 256, 256), 256)
        for at in range(0, CB, 256):
            some = jnp.dot(hot_b[:, group], pool_b[group, at:at + 256], preferred_element_type=F32)
            if o > 0:
                some = some + sum_b[:, at:at + 256]
            if last:
                picked[:, CA + at:CA + at + 256] = some.astype(BF16)
            else:
                sum_b[:, at:at + 256] = some

    half = PICKS // 2
    low, high = pl.ds(0, half), pl.ds(half, half)
    right, left, across = (x + 1) % X, (x + 3) % X, (x + 2) % X
    for event in ORDER:
        if event in coming:
            coming[event].wait_recv()
        kind = event[0]
        if kind == "A":
            on_a(*event[1:])
        elif kind == "B":
            on_b(*event[1:])
        elif kind == "Bx":
            on_bx(*event[1:])
        elif kind == "eig":
            loads[3].wait()
            total = jnp.zeros((8, 128), F32)
            for at in range(0, IB, 128):
                block = eigv[at:at + 128, :].astype(F32)
                for at_lane in range(0, JB, 128):
                    total = total + jnp.sum(block[:, at_lane:at_lane + 128].reshape(16, 8, 128), axis=0)
            damp = sum_start(damp_s, k, total, [sibling])
        elif kind == "hot_a":
            mark(hot_a, lambda at: ((at // 32) % 4) * 256 + (at // 128) * 32 + at % 32)
        elif kind == "hot_b":
            mark(hot_b, lambda at: at)
        elif kind == "hot_c":
            mark(hot_c, lambda at: ((at // 64) % 8) * 128 + (at // 512) * 64 + at % 64)
        elif kind == "pick_b":
            pick_b(event[1])
        elif kind == "damp_z":
            damp = sum_start(damp_z, z, sum_end(damp_s, damp), to_z)
        elif kind == "damp_y":
            damp = sum_start(damp_y, y, sum_end(damp_z, damp), to_y)
        elif kind == "damp_x":
            damp = sum_start(damp_x, x, sum_end(damp_y, damp), to_x)
        elif kind == "acts":
            for copy in c_z:
                copy.wait_recv()
            half_c = pl.ds(pl.multiple_of(k * 512, 512), 512)
            c_s = remote(pool_c.at[half_c], pool_c.at[half_c], sibling)
        elif kind == "in_rot":
            c_s.wait_recv()
            loads[4].wait()
            act_rows = jnp.dot(hot_c[...], pool_c[...], preferred_element_type=F32).astype(BF16)
            for at in range(X):
                in_part[at] = jnp.dot(
                    act_rows, ibv[:, at * 128:at * 128 + 128], preferred_element_type=F32
                )
        elif kind == "in_x":
            relays = [
                remote(in_part.at[across, low], in_relay.at[0], dev(ox=1)),
                remote(in_part.at[across, high], in_relay.at[1], dev(ox=-1)),
            ]
            in_copies = [
                remote(in_part.at[right, high], in_x.at[0, high], dev(ox=1)),
                remote(in_part.at[left, low], in_x.at[1, low], dev(ox=-1)),
            ]

    for at in range(0, CA, 256):
        picked[:, at:at + 256] = jnp.dot(
            hot_a[...], pool_a[:, at:at + 256], preferred_element_type=F32
        ).astype(BF16)
    pick_b(2, last=True)
    for copy in relays:
        copy.wait_recv()
    in_send[0] = in_relay[0] + in_part[right, low]
    in_send[1] = in_relay[1] + in_part[left, high]
    in_copies += [
        remote(in_send.at[0], in_x.at[0, low], dev(ox=1)),
        remote(in_send.at[1], in_x.at[1, high], dev(ox=-1)),
    ]

    def chunk(d):
        return rows(((d + 2 * Z) % Z) * CH, CH)

    loads[5].wait()
    swaps = [[] for _ in range(4)]
    for start, end in ((0, 512), (512, IB)):
        for at in range(start, end, 256):
            width = min(256, IB - at)
            rotated = jnp.dot(picked[...], obv[:, at:at + width], preferred_element_type=F32)
            for d in range(Z):
                part[d * CH:d * CH + TCH, at:at + width] = rotated[d * TCH:d * TCH + TCH]
                part[d * CH + TCH:d * CH + CH, at:at + width] = rotated[TRAIN:TRAIN + QUERIES]
        span = pl.ds(start, end - start)
        for j in range(4):
            need = jnp.where(k == 1, z + 4 - j, z if j == 0 else z - 4 + j)
            swaps[j].append(remote(part.at[chunk(need), span], swap.at[j, :, span], sibling))

    hops = []
    for s in range(4):
        for copy in swaps[s]:
            copy.wait_recv()
        mine = part.at[chunk(z + turn * (4 - s))]
        hop = []
        for p, (first, size) in enumerate(PARTS):
            span = pl.ds(first, size)
            if s > 0:
                if s == 1:
                    @pl.when(k == 0)
                    def _():
                        hops[0][p].wait_recv()
                else:
                    hops[s - 1][p].wait_recv()
                sendbuf[s, span] = mine[span] + swap[s, span] + ringbuf[s - 1, span]
            else:
                sendbuf[s, span] = mine[span] + swap[s, span]
            copy = remote(
                sendbuf.at[s, span], ringbuf.at[s, span], dev(oz=turn), start=s > 0
            )
            if s == 0:
                @pl.when(k == 0)
                def _():
                    copy.start()
            hop.append(copy)
        hops.append(hop)
        if s == 0:
            for copy in in_copies:
                copy.wait_recv()
            sums = in_part[x] + in_x[0] + in_x[1]
            for d in range(Y):
                in_sum[d, 0:TCH] = sums[d * TCH:d * TCH + TCH]
                in_sum[d, TCH:CH] = sums[TRAIN:TRAIN + QUERIES]
            in_copies = [
                remote(in_sum.at[(y + o) % Y], in_y.at[o - 1], dev(oy=o)) for o in range(1, Y)
            ]
        if s == 2:
            damping = 0.1 * jnp.sum(sum_end(damp_x, damp)) / (DOUT * DIN)
            inverse[...] = 1.0 / (eigv[...].astype(F32) + damping)

    def in_middle():
        for copy in in_copies:
            copy.wait_recv()
        sums = in_sum[y]
        for o in range(1, Y):
            sums = sums + in_y[o - 1]
        rin[x, pl.ds(pl.multiple_of(y * TCH, 16), TCH)] = sums[0:TCH].astype(BF16)
        span = pl.ds(pl.multiple_of(y * TCH, 16), TCH)
        rin_query[x] = sums[TCH:CH].astype(BF16).astype(F32)
        return (
            [remote(rin.at[x, span], rin.at[x, span], dev(oy=o)) for o in range(1, Y)],
            [remote(rin_query.at[x], rin_query.at[x], dev(ox=o)) for o in range(1, X)],
        )

    in_copies, in_queries = in_middle()
    meets = []
    for p, (first, size) in enumerate(PARTS):
        span = pl.ds(first, size)
        hops[3][p].wait_recv()
        rest = part[rows(z * CH + first, size)] + swap[0, span]
        own[span] = ringbuf[3, span] + jnp.where(k == 1, rest, 0.0)
        meets.append(remote(own.at[span], own_other.at[span], sibling))

    def chunk_rows(o, first=0, size=TCH):
        return pl.ds(pl.multiple_of(((z - turn * o + 2 * Z) % Z) * TCH + first, 16), size)

    spread = {}
    for p, (first, size) in enumerate(PARTS):
        span = pl.ds(first, size)
        meets[p].wait_recv()
        full = own[span] + own_other[span]
        if size > 16:
            rquery[...] = full[16:24].astype(BF16).astype(F32)
        where = chunk_rows(0, first, 16)
        rout[where] = full[0:16].astype(BF16)
        for o in (3, 2, 1):
            spread[o, p] = remote(rout.at[where], rout.at[where], dev(oz=turn * o))

    for copy in in_queries:
        copy.wait_recv()
    query_columns = jnp.transpose(rquery[...])
    for q in range(QUERIES):
        column = query_columns[:, q:q + 1]
        for t in range(X):
            cols = slice(t * 128, t * 128 + 128)
            precond[q, :, cols] = (column * rin_query[t, q:q + 1] * inverse[:, cols]).astype(BF16)

    for copy in in_copies:
        copy.wait_recv()
    in_right = remote(rin.at[x], rin.at[x], dev(ox=1))
    in_left = remote(rin.at[x], rin.at[x], dev(ox=-1))

    far = []
    for p, (first, _) in enumerate(PARTS):
        core = 0 if p < 2 else 1
        spread[3, p].wait_recv()
        where = chunk_rows(3, first, 16)
        copy = remote(rout.at[where], rout.at[where], dev(oz=turn), start=False)
        far.append((core, first, 16, copy))

        @pl.when(k == core)
        def _():
            copy.start()
        spread[2, p].wait_recv()
        spread[1, p].wait_recv()
        if p == 1:
            in_right.wait_recv()
            in_cross = [
                remote(rin.at[left, pl.ds(0, 192)], rin.at[left, pl.ds(0, 192)], dev(ox=1)),
            ]
            in_left.wait_recv()
            in_cross += [
                remote(rin.at[right, pl.ds(192, 192)], rin.at[right, pl.ds(192, 192)], dev(ox=-1)),
            ]
    relayed = [remote(rout.at[chunk_rows(o)], rout.at[chunk_rows(o)], sibling) for o in (1, 2, 3)]
    late = []
    for core, first, size, copy in far:
        relay = remote(
            rout.at[chunk_rows(4, first, size)], rout.at[chunk_rows(4, first, size)], sibling, start=False
        )
        late.append((core, copy, relay))

        @pl.when(k == core)
        def _():
            copy.wait_recv()
            relay.start()
    for copy in in_cross + relayed:
        copy.wait_recv()
    for core, copy, relay in late:
        @pl.when(k != core)
        def _():
            relay.wait_recv()

    lanes = lax.broadcasted_iota(jnp.int32, (TRAIN, 128), 1)
    collected = jnp.zeros((TRAIN, 128), F32)
    for q in range(QUERIES):
        total = jnp.zeros((TRAIN, 128), F32)
        for at in range(0, X, 2):
            mixed = jnp.dot(
                rout[...], precond[q, :, at * 128:at * 128 + 256], preferred_element_type=F32
            )
            for n, t in enumerate((at, at + 1)):
                total = total + mixed[:, n * 128:n * 128 + 128] * rin[t].astype(F32)
        collected = jnp.where(lanes == q, jnp.sum(total, axis=1, keepdims=True), collected)
    scores = jnp.transpose(collected)[0:QUERIES]

    assert used[0] + 25 <= N_SEM
    fin = sum_start(fin_s, k, scores, [sibling])
    fin = sum_start(fin_z, z, sum_end(fin_s, fin), to_z)
    fin = sum_start(fin_y, y, sum_end(fin_z, fin), to_y)
    fin = sum_start(fin_x, x, sum_end(fin_y, fin), to_x)
    out[...] = sum_end(fin_x, fin)

    for copy in pending:
        copy.wait_send()

    @pl.when(k == 0)
    def _():
        for copy in hops[0]:
            copy.wait_send()
    for core, copy, relay in late:
        @pl.when(k == core)
        def _():
            copy.wait_send()
            relay.wait_send()


def per_device(grads_out, acts, query_index, train_index, out_basis, in_basis, eig_products):
    vmem = pl.BlockSpec(memory_space=pltpu.VMEM)
    hbm = pl.BlockSpec(memory_space=pl.ANY)
    scores = pl.pallas_call(
        kernel,
        out_shape=jax.ShapeDtypeStruct((QUERIES, TRAIN), F32),
        in_specs=[vmem, pl.BlockSpec(memory_space=pltpu.SMEM)] + [hbm] * 5,
        out_specs=vmem,
        scratch_shapes=[
            pltpu.VMEM((PICKS, 1), jnp.int32),
            pltpu.VMEM((POOL, CA), BF16),
            pltpu.VMEM((POOL, CB), BF16),
            pltpu.VMEM((POOL, 256), BF16),
            pltpu.VMEM((PICKS, CB), F32),
            pltpu.VMEM((PICKS, POOL), BF16),
            pltpu.VMEM((PICKS, POOL), BF16),
            pltpu.VMEM((PICKS, POOL), BF16),
            pltpu.VMEM((CA + CB, IB), BF16),
            pltpu.VMEM((256, JB), BF16),
            pltpu.VMEM((IB, JB), BF16),
            pltpu.VMEM((IB, JB), F32),
            pltpu.VMEM((PICKS, CA + CB), BF16),
            pltpu.VMEM((Z * CH, IB), F32),
            pltpu.VMEM((4, CH, IB), F32),
            pltpu.VMEM((4, CH, IB), F32),
            pltpu.VMEM((4, CH, IB), F32),
            pltpu.VMEM((CH, IB), F32),
            pltpu.VMEM((CH, IB), F32),
            pltpu.VMEM((TRAIN, IB), BF16),
            pltpu.VMEM((QUERIES, IB), F32),
            pltpu.VMEM((X, PICKS, 128), F32),
            pltpu.VMEM((2, PICKS // 2, 128), F32),
            pltpu.VMEM((2, PICKS // 2, 128), F32),
            pltpu.VMEM((2, PICKS, 128), F32),
            pltpu.VMEM((Y, CH, 128), F32),
            pltpu.VMEM((Y - 1, CH, 128), F32),
            pltpu.VMEM((X, TRAIN, 128), BF16),
            pltpu.VMEM((X, QUERIES, 128), F32),
            pltpu.VMEM((QUERIES, IB, JB), BF16),
            pltpu.VMEM((2, 8, 128), F32),
            pltpu.VMEM((Z, 8, 128), F32),
            pltpu.VMEM((Y, 8, 128), F32),
            pltpu.VMEM((X, 8, 128), F32),
            pltpu.VMEM((2, QUERIES, TRAIN), F32),
            pltpu.VMEM((Z, QUERIES, TRAIN), F32),
            pltpu.VMEM((Y, QUERIES, TRAIN), F32),
            pltpu.VMEM((X, QUERIES, TRAIN), F32),
            pltpu.SemaphoreType.DMA((N_SEM,)),
            pltpu.SemaphoreType.DMA((N_SEM,)),
            pltpu.SemaphoreType.DMA((6,)),
        ],
        compiler_params=pltpu.CompilerParams(
            collective_id=0, has_side_effects=True, vmem_limit_bytes=56 * 2**20
        ),
    )(train_index, query_index, grads_out, acts, out_basis, in_basis, eig_products)
    return scores * (1.0 / math.sqrt(DOUT * DIN))


def solution(mesh):
    in_specs = (
        P("row", "col"),
        P("col", "row"),
        P(),
        P(),
        P("col", "row"),
        P("row", "col"),
        P("row", "col"),
    )
    return jax.shard_map(
        per_device, mesh=mesh, in_specs=in_specs, out_specs=P(), check_vma=False
    )
```

time: 102 us -> 95.7 us (0.938)
  Pallas kernels: 98.4 us -> 94.1 us
  local copies, waits for them, and re-layouts: 2.13 us -> 0 us
    pallas_call x1, Pallas kernels: 98.4 us -> 94.1 us  [per_device(): pl.pallas_call(kernel, out_shape=jax.ShapeDtypeStruct((QUERIES, TRAIN), F...]
    mul x0 -> x1, other arithmetic: none -> 1.31 us  [per_device(): return scores * (1.0 / math.sqrt(DOUT * DIN))]
    unnamed x1 -> x0, local copies, waits for them, and re-layouts: 1.31 us -> none
where the time goes in v2:
time: 95.7 us; the launch traced here: 95.5 us
  Pallas kernels  94.1 us (98%)
  other arithmetic  1.31 us (1%)
    pallas_call x1, Pallas kernels, per_device(): pl.pallas_call(kernel, out_shape=jax.ShapeDtypeStruct((QUERIES, TRAIN), F...  94.1 us

profile of v2, /device:TPU:1, one launch (start us, length us, event | category | flops | bytes accessed | tf_op | source)
XLA Modules:
  0.0 95.5 jit_solution(13837130865343426561)
XLA Ops:
  0.0 94.1 %shard_map.73 = f32[8,384]{1,0:T(8,128)} custom-call(s32[384]{0:T(512)} %train_index.1, s32[8]{0:T(128)} %query_index.1, bf16[32,1792]{1,0:T(8,128)(2,1)} %grads.1, bf16[64,256]{1,0:T(8,128)(2,1)} %acts.1, bf16[1792,896]{1,0:T(8,128)(2,1)} %out_basis.1, bf16[256,512]{1,0:T(8,128)(2,1)} %in_basis.1, bf16[896,512]{1,0:T(8,128)(2,1)} %eig.1), custom_call_target="tpu_custom_call" | custom-call | tf_op jit(solution)/shard_map/pallas_call | solution.py:459
  94.2 1.3 %broadcast_multiply_fusion = f32[8,384]{1,0:T(8,128)} fusion(f32[8,384]{1,0:T(8,128)} %shard_map.73), kind=kLoop, calls=%fused_computation | loop fusion | flops 3072 | bytes 24576 | tf_op jit(solution)/shard_map/mul | solution.py:511

commit v3 on v2

--- a/solution.py
+++ b/solution.py
@@ -23,6 +23,8 @@
 MESH = pl.DeviceIdType.MESH
 F32 = jnp.float32
 BF16 = jnp.bfloat16
+FAR8 = (4, 3, 5, 2, 6, 1, 7)
+FAR4 = (2, 1, 3)
 PARTS = ((0, 16), (16, 16), (32, 24))
 N_SEM = 208
 ORDER = (
@@ -44,7 +46,7 @@
     train_index, query_index, grads, acts, out_basis, in_basis, eig, out,
     want_rows, pool_a, pool_b, pool_c, sum_b, hot_a, hot_b, hot_c, obv, ibv, eigv, inverse, picked,
     part, swap, ringbuf, sendbuf, own, own_other, rout, rquery,
-    in_part, in_relay, in_send, in_x, in_sum, in_y, rin, rin_query, precond, damp_s, damp_z, damp_y, damp_x,
+    in_part, in_relay, in_send, in_x, in_sum, in_y, rin, rin_query, precond, mixed, damp_s, damp_z, damp_y, damp_x,
     fin_s, fin_z, fin_y, fin_x, send_sems, recv_sems, load_sems,
 ):
     row = lax.axis_index("row")
@@ -77,10 +79,8 @@
         return pl.ds(pl.multiple_of(start, 8), size)
 
     barrier = pltpu.get_barrier_semaphore()
-    partners = [sibling]
-    partners += [dev(oz=o) for o in range(1, Z)]
-    partners += [dev(oy=o) for o in range(1, Y)]
-    partners += [dev(ox=o) for o in range(1, X)]
+    partners = [dev(oz=o) for o in FAR8] + [dev(oy=o) for o in FAR8] + [dev(ox=o) for o in FAR4]
+    partners += [sibling]
     for partner in partners:
         pl.semaphore_signal(barrier, inc=1, device_id=partner, device_id_type=MESH)
 
@@ -169,9 +169,9 @@
             result = result + buf[at]
         return result
 
-    to_z = [dev(oz=o) for o in range(1, Z)]
-    to_y = [dev(oy=o) for o in range(1, Y)]
-    to_x = [dev(ox=o) for o in range(1, X)]
+    to_z = [dev(oz=o) for o in FAR8]
+    to_y = [dev(oy=o) for o in FAR8]
+    to_x = [dev(ox=o) for o in FAR4]
 
     train_line = jnp.broadcast_to(train_index[...].reshape(1, TRAIN).astype(F32), (8, TRAIN))
     want_rows[0:TRAIN] = jnp.transpose(train_line)[:, 0:1].astype(jnp.int32)
@@ -320,7 +320,7 @@
                 in_sum[d, 0:TCH] = sums[d * TCH:d * TCH + TCH]
                 in_sum[d, TCH:CH] = sums[TRAIN:TRAIN + QUERIES]
             in_copies = [
-                remote(in_sum.at[(y + o) % Y], in_y.at[o - 1], dev(oy=o)) for o in range(1, Y)
+                remote(in_sum.at[(y + o) % Y], in_y.at[o - 1], dev(oy=o)) for o in FAR8
             ]
         if s == 2:
             damping = 0.1 * jnp.sum(sum_end(damp_x, damp)) / (DOUT * DIN)
@@ -336,8 +336,8 @@
         span = pl.ds(pl.multiple_of(y * TCH, 16), TCH)
         rin_query[x] = sums[TCH:CH].astype(BF16).astype(F32)
         return (
-            [remote(rin.at[x, span], rin.at[x, span], dev(oy=o)) for o in range(1, Y)],
-            [remote(rin_query.at[x], rin_query.at[x], dev(ox=o)) for o in range(1, X)],
+            [remote(rin.at[x, span], rin.at[x, span], dev(oy=o)) for o in FAR8],
+            [remote(rin_query.at[x], rin_query.at[x], dev(ox=o)) for o in FAR4],
         )
 
     in_copies, in_queries = in_middle()
@@ -391,16 +391,15 @@
             copy.start()
         spread[2, p].wait_recv()
         spread[1, p].wait_recv()
-        if p == 1:
-            in_right.wait_recv()
-            in_cross = [
-                remote(rin.at[left, pl.ds(0, 192)], rin.at[left, pl.ds(0, 192)], dev(ox=1)),
-            ]
-            in_left.wait_recv()
-            in_cross += [
-                remote(rin.at[right, pl.ds(192, 192)], rin.at[right, pl.ds(192, 192)], dev(ox=-1)),
-            ]
     relayed = [remote(rout.at[chunk_rows(o)], rout.at[chunk_rows(o)], sibling) for o in (1, 2, 3)]
+    in_right.wait_recv()
+    in_cross = [
+        remote(rin.at[left, pl.ds(0, 192)], rin.at[left, pl.ds(0, 192)], dev(ox=1)),
+    ]
+    in_left.wait_recv()
+    in_cross += [
+        remote(rin.at[right, pl.ds(192, 192)], rin.at[right, pl.ds(192, 192)], dev(ox=-1)),
+    ]
     late = []
     for core, first, size, copy in far:
         relay = remote(
@@ -412,23 +411,26 @@
         def _():
             copy.wait_recv()
             relay.start()
-    for copy in in_cross + relayed:
+    for copy in relayed:
         copy.wait_recv()
     for core, copy, relay in late:
         @pl.when(k != core)
         def _():
             relay.wait_recv()
 
+    for q in range(QUERIES):
+        for at in range(0, JB, 256):
+            mixed[q, :, at:at + 256] = jnp.dot(
+                rout[...], precond[q, :, at:at + 256], preferred_element_type=F32
+            )
+    for copy in in_cross:
+        copy.wait_recv()
     lanes = lax.broadcasted_iota(jnp.int32, (TRAIN, 128), 1)
     collected = jnp.zeros((TRAIN, 128), F32)
     for q in range(QUERIES):
         total = jnp.zeros((TRAIN, 128), F32)
-        for at in range(0, X, 2):
-            mixed = jnp.dot(
-                rout[...], precond[q, :, at * 128:at * 128 + 256], preferred_element_type=F32
-            )
-            for n, t in enumerate((at, at + 1)):
-                total = total + mixed[:, n * 128:n * 128 + 128] * rin[t].astype(F32)
+        for t in range(X):
+            total = total + mixed[q, :, t * 128:t * 128 + 128] * rin[t].astype(F32)
         collected = jnp.where(lanes == q, jnp.sum(total, axis=1, keepdims=True), collected)
     scores = jnp.transpose(collected)[0:QUERIES]
 
@@ -492,6 +494,7 @@
             pltpu.VMEM((X, TRAIN, 128), BF16),
             pltpu.VMEM((X, QUERIES, 128), F32),
             pltpu.VMEM((QUERIES, IB, JB), BF16),
+            pltpu.VMEM((QUERIES, TRAIN, JB), F32),
             pltpu.VMEM((2, 8, 128), F32),
             pltpu.VMEM((Z, 8, 128), F32),
             pltpu.VMEM((Y, 8, 128), F32),

time: 95.7 us -> 95 us (level)
  the two profiles are of different devices: /device:TPU:1 before, /device:TPU:8 now
where the time goes in v3:
time: 95 us; the launch traced here: 94.8 us
  Pallas kernels  93.5 us (98%)
  other arithmetic  1.31 us (1%)
    pallas_call x1, Pallas kernels, per_device(): pl.pallas_call(kernel, out_shape=jax.ShapeDtypeStruct((QUERIES, TRAIN), F...  93.5 us

profile of v3, /device:TPU:8, one launch (start us, length us, event | category | flops | bytes accessed | tf_op | source)
XLA Modules:
  0.0 94.8 jit_solution(6499849514083290451)
XLA Ops:
  0.0 93.5 %shard_map.73 = f32[8,384]{1,0:T(8,128)} custom-call(s32[384]{0:T(512)} %train_index.1, s32[8]{0:T(128)} %query_index.1, bf16[32,1792]{1,0:T(8,128)(2,1)} %grads.1, bf16[64,256]{1,0:T(8,128)(2,1)} %acts.1, bf16[1792,896]{1,0:T(8,128)(2,1)} %out_basis.1, bf16[256,512]{1,0:T(8,128)(2,1)} %in_basis.1, bf16[896,512]{1,0:T(8,128)(2,1)} %eig.1), custom_call_target="tpu_custom_call" | custom-call | tf_op jit(solution)/shard_map/pallas_call | solution.py:461
  93.5 1.3 %broadcast_multiply_fusion = f32[8,384]{1,0:T(8,128)} fusion(f32[8,384]{1,0:T(8,128)} %shard_map.73), kind=kLoop, calls=%fused_computation | loop fusion | flops 3072 | bytes 24576 | tf_op jit(solution)/shard_map/mul | solution.py:514
